TPU v7x, 512 devices: a whole 4x8x8 slice. The times are simulated.
512 devices in a mesh: dp: 64 (over y, x, core), mp: 8 (over z).
Axes of the slice: x: 4, y: 8, z: 8, core: 2. Of those that a mesh axis runs over, the one named last changes fastest.
Arguments:
- activations: bfloat16 [32768, 8192], P('dp', 'mp'), may hold values from -16 to 16
- cotangent: bfloat16 [32768, 8192], P('dp', 'mp'), may hold values from -0.099121094 to 0.099121094
- basis: bfloat16 [8192, 1024], P('mp'), may hold values from -0.0625 to 0.0625
- weight: bfloat16 [8192, 8192], P(('mp', 'dp')), may hold values from -3 to 3
- first_moment: float32 [8192, 1024], P(('mp', 'dp')), may hold values from -3 to 3
- second_moment: float32 [8192, 1024], P(('mp', 'dp')), may hold values from 0.05 to 2
Outputs:
- new_weight: bfloat16 [8192, 8192], P(('mp', 'dp'))
- new_first: float32 [8192, 1024], P(('mp', 'dp'))
- new_second: float32 [8192, 1024], P(('mp', 'dp'))
All inputs are finite; a program needn't handle non-finite values.
Results may differ from a plain program's by a relative error of at most 0.002.
Values may be sent and summed in bfloat16 or wider, within the bound.
A program may use at most 64 MiB of HBM per device.

v0:
```python
import jax
import jax.numpy as jnp
from jax import lax
from jax.sharding import PartitionSpec as P

STEP = 1000


beta_first = 0.9
beta_second = 0.999
adam_eps = 1e-08
step_rate = 0.1


def body(activations, cotangent, basis, weight, first_moment, second_moment):
    partial_value = jnp.dot(cotangent, basis, preferred_element_type=jnp.float32)
    projected = lax.psum(partial_value, "mp").astype(jnp.bfloat16)
    grad = lax.psum_scatter(
        lax.dot_general(
            activations, projected, (((0,), (0,)), ((), ())), preferred_element_type=jnp.float32
        ),
        "dp",
        scatter_dimension=0,
        tiled=True,
    )
    new_first = beta_first * first_moment + (1.0 - beta_first) * grad
    new_second = beta_second * second_moment + (1.0 - beta_second) * grad * grad
    first_hat = new_first / (1.0 - beta_first**STEP)
    second_hat = new_second / (1.0 - beta_second**STEP)
    low_rank = (first_hat / (jnp.sqrt(second_hat) + adam_eps)).astype(jnp.bfloat16)
    blocks = lax.dot_general(
        lax.all_gather(low_rank, "mp", axis=0, tiled=True),
        basis,
        (((1,), (1,)), ((), ())),
        preferred_element_type=jnp.float32,
    ).astype(jnp.bfloat16)
    delta = lax.all_to_all(blocks, "mp", split_axis=0, concat_axis=1, tiled=True)
    new_weight = (weight.astype(jnp.float32) - step_rate * delta.astype(jnp.float32)).astype(
        jnp.bfloat16
    )
    return (new_weight, new_first, new_second)


def solution(mesh):
    placed = (
        P("dp", "mp"),
        P("dp", "mp"),
        P("mp", None),
        P(("mp", "dp"), None),
        P(("mp", "dp"), None),
        P(("mp", "dp"), None),
    )
    return jax.shard_map(
        body,
        mesh=mesh,
        in_specs=placed,
        out_specs=(P(("mp", "dp"), None), P(("mp", "dp"), None), P(("mp", "dp"), None)),
        check_vma=False,
    )
```

profile of v0, /device:TPU:16, one launch (start us, length us, event | category | flops | bytes accessed | tf_op | source)
XLA Modules:
  0.0 297.9 jit_solution(13051556545980239288)
XLA Ops:
  7.2 0.0 copy-start
  7.2 0.0 reduce-scatter.4.cloned.1.call-start
  7.2 1.5 copy-done
  8.8 3.8 %fusion.3 = f32[512,1024]{1,0:T(8,128)} fusion(bf16[512,1024]{1,0:T(8,128)(2,1)} %param.7, bf16[1024,1024]{1,0:T(8,128)(2,1)S(1)} %copy-done), kind=kOutput, calls=%fused_computation.9 | convolution fusion | flops 1073741824 | bytes 5242880 | tf_op jit(solution)/shard_map/dot_general | solution.py:16
  12.6 73.5 %all-reduce.1 = bf16[512,1024]{1,0:T(8,128)(2,1)S(1)} all-reduce(f32[512,1024]{1,0:T(8,128)} %fusion.3), channel_id=1, replica_groups=mesh['dp'=64,'mp'=8] {'mp'}, use_global_device_ids=true, to_apply=%region_0.0 | all-reduce | flops 524288 | bytes 3145728 | tf_op jit(solution)/shard_map/psum | solution.py:17
  86.1 4.5 %convolution_bitcast_fusion = f32[1024,1024]{0,1:T(8,128)} fusion(bf16[512,1024]{1,0:T(8,128)(2,1)} %param.6, bf16[512,1024]{1,0:T(8,128)(2,1)S(1)} %all-reduce.1), kind=kOutput, calls=%fused_computation | convolution fusion | flops 1073741824 | bytes 6291456 | tf_op jit(solution)/shard_map/dot_general | solution.py:19
  90.6 5.3 %copy.28 = f32[1024,1024]{1,0:T(8,128)} copy(f32[1024,1024]{0,1:T(8,128)} %convolution_bitcast_fusion) | data formatting | bytes 8388608
  95.9 0.0 copy-start.2
  95.9 0.0 copy-start.3
  95.9 0.0 reduce-scatter.4.cloned.1.call-update
  95.9 148.8 %reduce-scatter.4.cloned.1.call-done = f32[16,1024]{1,0:T(8,128)} async-done(((f32[1024,1024]{1,0:T(8,128)}), f32[16,1024]{1,0:T(8,128)}) %reduce-scatter.4.cloned.1.call-update) | async-done | bytes 65552 | tf_op jit(solution)/shard_map/reduce_scatter | solution.py:18
  244.8 0.0 copy-done.2
  244.8 0.0 copy-done.3
  244.8 1.5 divide_convert_fusion
  246.3 27.7 %all_gather.3 = bf16[128,1024]{1,0:T(8,128)(2,1)S(1)} all-gather(bf16[16,1024]{1,0:T(8,128)(2,1)S(1)} %get-tuple-element.9), channel_id=1, replica_groups=mesh['dp'=64,'mp'=8] {'mp'}, dimensions={0}, use_global_device_ids=true | all-gather | bytes 294912 | tf_op jit(solution)/shard_map/all_gather | solution.py:32
  274.0 0.0 copy-start.1
  274.0 0.8 convolution_convert_fusion
  274.8 15.4 %all_to_all.13 = bf16[8,16,1024]{2,1,0:T(8,128)(2,1)S(1)} all-to-all(bf16[8,16,1024]{2,1,0:T(8,128)(2,1)S(1)} %bitcast.15), channel_id=1, replica_groups=mesh['dp'=64,'mp'=8] {'mp'}, dimensions={0} | all-to-all | bytes 524288 | tf_op jit(solution)/shard_map/all_to_all | solution.py:37
  290.3 0.0 copy-done.1
  290.3 0.8 subtract_convert_fusion
  (2 shorter events, 0.1 us)
Async XLA Ops:
  7.2 1.6 copy-start
  7.2 237.6 %reduce-scatter.4.cloned.1.call-start = ((), (), s32[]{:S(2)}) async-start(), calls=%async_computation.2 | async-start | bytes 4259840 | tf_op jit(solution)/shard_map/reduce_scatter | solution.py:18
  95.9 148.9 %copy-start.2 = (f32[16,1024]{1,0:T(8,128)S(1)}, f32[16,1024]{1,0:T(8,128)}, u32[]{:S(2)}) copy-start(f32[16,1024]{1,0:T(8,128)} %param.11) | copy-start | bytes 196612
  95.9 148.9 %copy-start.3 = (f32[16,1024]{1,0:T(8,128)S(1)}, f32[16,1024]{1,0:T(8,128)}, u32[]{:S(2)}) copy-start(f32[16,1024]{1,0:T(8,128)} %param.10) | copy-start | bytes 196612
  274.0 16.3 %copy-start.1 = (bf16[16,8192]{1,0:T(8,128)(2,1)S(1)}, bf16[16,8192]{1,0:T(8,128)(2,1)}, u32[]{:S(2)}) copy-start(bf16[16,8192]{1,0:T(8,128)(2,1)} %param.9) | copy-start | bytes 786436
Sparse Core Ops, SparseCore 0:
  96.1 148.6 reduce-scatter.3
where the time goes:
time: 298 us
  waiting for transfers between devices  149 us (50%)
  blocking collectives  117 us (39%)
  between operations  14.1 us (5%)
  matrix products  9.13 us (3%)
  local copies, waits for them, and re-layouts  6.94 us (2%)
    reduce_scatter x1, waiting for transfers between devices, body(): lax.psum_scatter(lax.dot_general(activations, projected, (((0,), (0,)), (...  149 us
    psum x1, blocking collectives, body(): projected = lax.psum(partial_value, 'mp').astype(jnp.bfloat16)  73.5 us
    all_gather x1, blocking collectives, body(): lax.all_gather(low_rank, 'mp', axis=0, tiled=True)  27.7 us
    all_to_all x1, blocking collectives, body(): lax.all_to_all(blocks, 'mp', split_axis=0, concat_axis=1, tiled=True)  15.4 us
    unnamed x9, local copies, waits for them, and re-layouts  6.9 us
  transfers between devices with their start and end apart: 1, of which 1 were waited for; matrix products, arithmetic and copies ran while one was open for 0% of the time, Pallas kernels for 0%

commit v1 on v0

v1 whole, which is shorter than its diff:
```python
import jax
import jax.numpy as jnp
from jax import lax
from jax.experimental import pallas as pl
from jax.experimental.pallas import tpu as pltpu
from jax.sharding import PartitionSpec as P

STEP = 1000

beta_first = 0.9
beta_second = 0.999
adam_eps = 1e-08
step_rate = 0.1

MESH = pl.DeviceIdType.MESH
F32, BF16 = jnp.float32, jnp.bfloat16

PARENT = {4: 3, 3: 1, 2: 1, 1: 0, -3: -2, -2: -1, -1: 0}
SLOT = {o: i for i, o in enumerate(PARENT)}
CHUNKS = 4
WIDTH = 1024 // CHUNKS
LIFT = 2.0**24


def children(node):
    return [o for o in PARENT if PARENT[o] == node]


def height(node):
    return 1 + max([height(o) for o in children(node)], default=-1)


def depth(node):
    return 0 if node == 0 else 1 + depth(PARENT[node])


def encode(value):
    return ((value * value) * (value * jnp.abs(value))).astype(BF16)


def decode(code):
    code = code.astype(F32)
    root = lax.rsqrt(jnp.maximum(jnp.abs(code), 1e-37))
    return code * (root * root) * lax.rsqrt(root)


def each(function):
    lax.fori_loop(0, CHUNKS, lambda c, carry: (function(c), carry)[1], 0)


def kernel(
    act_in, cot_in, basis_in, weight_in, first_in, second_in,
    weight_out, first_out, second_out,
    act, cot, basis, weight, first, second,
    partial, rs_send, rs_recv, proj, act_t, own, core_send, core_recv,
    x_send, x_recv, y_sum, y_send, y_recv, low, total, d_send, d_recv,
    load_sem, rs_ss, rs_rs, ag_ss, ag_rs, core_ss, core_rs, x_ss, x_rs, y_ss, y_rs, low_ss, low_rs, d_ss, d_rs,
):
    dp, z = lax.axis_index("dp"), lax.axis_index("mp")
    y, x, core = dp // 8, (dp // 2) % 4, dp % 2
    sign = 1 - 2 * core

    def along_z(offset):
        return lax.rem(z + sign * offset + 16, 8)

    def at(y_to, x_to, core_to, z_to):
        return ((y_to * 4 + x_to) * 2 + core_to, z_to)

    def z_peer(offset):
        return at(y, x, core, along_z(offset))

    def x_peer(k):
        return at(y, lax.rem(x + k, 4), core, z)

    def y_peer(k):
        return at(lax.rem(y + k, 8), x, core, z)

    core_peer = at(y, x, 1 - core, z)

    def columns(c):
        return pl.ds(pl.multiple_of(c * WIDTH, WIDTH), WIDTH)

    def load(i, source, target):
        return pltpu.make_async_copy(source, target, load_sem.at[i])

    cot_load = load(0, cot_in, cot)
    act_load = load(1, act_in, act)
    weight_load = load(2, weight_in, weight)
    first_load = load(3, first_in, first)
    second_load = load(4, second_in, second)

    def basis_load(c):
        return load(5 + c, basis_in.at[:, columns(c)], basis.at[c])

    cot_load.start()
    each(lambda c: basis_load(c).start())
    act_load.start()
    first_load.start()
    second_load.start()
    weight_load.start()

    barrier = pltpu.get_barrier_semaphore()
    peers = [z_peer(k) for k in range(1, 8)] + [x_peer(k) for k in range(1, 4)]
    peers += [y_peer(k) for k in range(1, 8)] + [core_peer]
    for peer in peers:
        pl.semaphore_signal(barrier, inc=1, device_id=peer, device_id_type=MESH)

    def send(source, target, send_sem, recv_sem, peer):
        return pltpu.make_async_remote_copy(
            src_ref=source,
            dst_ref=target,
            send_sem=send_sem,
            recv_sem=recv_sem,
            device_id=peer,
            device_id_type=MESH,
        )

    def rs_copy(c, o):
        i = SLOT[o]
        return send(rs_send.at[c, i], rs_recv.at[c, i], rs_ss.at[c, i], rs_rs.at[c, i], z_peer(PARENT[o] - o))

    def ag_copy(c, o):
        i, block = SLOT[o], along_z(-PARENT[o])
        return send(
            proj.at[c, block], proj.at[c, block], ag_ss.at[c, i], ag_rs.at[c, i], z_peer(o - PARENT[o])
        )

    def core_copy(c):
        return send(core_send.at[c], core_recv.at[c], core_ss.at[c], core_rs.at[c], core_peer)

    def x_copy(c, k):
        return send(x_send.at[c, k - 1], x_recv.at[c, k - 1], x_ss.at[c, k - 1], x_rs.at[c, k - 1], x_peer(k))

    def y_copy(c, k):
        return send(y_send.at[c, k - 1], y_recv.at[c, k - 1], y_ss.at[c, k - 1], y_rs.at[c, k - 1], y_peer(k))

    def low_copy(c, k):
        return send(low.at[c, z], low.at[c, z], low_ss.at[c, k - 1], low_rs.at[c, k - 1], z_peer(k))

    def d_copy(k):
        return send(d_send.at[along_z(k)], d_recv.at[k - 1], d_ss.at[k - 1], d_rs.at[k - 1], z_peer(k))

    def rs_step(c, o):
        value = partial[c, along_z(-o)]
        for child in children(o):
            rs_copy(c, child).wait_recv()
            value += decode(rs_recv[c, SLOT[child]])
        rs_send[c, SLOT[o]] = encode(value)
        rs_copy(c, o).start()

    cot_load.wait()

    def multiply(c):
        basis_load(c).wait()
        product = jnp.dot(cot[...], basis[c], preferred_element_type=F32)
        partial[c] = (product * LIFT).reshape(8, 64, WIDTH)

    multiply(0)
    pl.semaphore_wait(barrier, len(peers))

    def first_sends(c):
        @pl.when(c > 0)
        def _():
            multiply(c)

        for o in PARENT:
            if height(o) == 0:
                rs_step(c, o)

    each(first_sends)

    act_load.wait()

    def transpose(i):
        block = act[:, pl.ds(pl.multiple_of(i * 128, 128), 128)].T.reshape(4, 2, 16, 512)
        for j in range(4):
            for k in range(2):
                act_t[k, j, i] = block[j, k]

    lax.fori_loop(0, 8, lambda i, carry: (transpose(i), carry)[1], 0)

    for level in range(1, height(0)):

        def later_sends(c):
            for o in PARENT:
                if height(o) == level:
                    rs_step(c, o)

        each(later_sends)

    def own_block(c):
        value = partial[c, z]
        for child in children(0):
            rs_copy(c, child).wait_recv()
            value += decode(rs_recv[c, SLOT[child]])
        proj[c, z] = (value * (1.0 / LIFT)).astype(BF16)
        for o in children(0):
            ag_copy(c, o).start()

    each(own_block)

    def received(c, o):
        ag_copy(c, o).wait_recv()

    for level in range(1, 1 + max(depth(o) for o in PARENT)):

        def forward(c):
            for o in PARENT:
                if depth(o) == level:
                    received(c, o)
                    for child in children(o):
                        ag_copy(c, child).start()

        each(forward)

    def gradient(c):
        here = proj[c].reshape(512, WIDTH)
        core_send[c] = jnp.dot(act_t[1 - core].reshape(512, 512), here, preferred_element_type=F32).reshape(4, 128, WIDTH)
        core_copy(c).start()
        own[c] = jnp.dot(act_t[core].reshape(512, 512), here, preferred_element_type=F32).reshape(4, 128, WIDTH)

    each(gradient)

    def over_x(c):
        core_copy(c).wait_recv()
        for k in (2, 1, 3):
            to = lax.rem(x + k, 4)
            x_send[c, k - 1] = encode(own[c, to] + core_recv[c, to])
            x_copy(c, k).start()

    each(over_x)

    def over_y(c):
        value = own[c, x] + core_recv[c, x]
        for k in range(1, 4):
            x_copy(c, k).wait_recv()
            value += decode(x_recv[c, k - 1])
        y_sum[c] = value.reshape(8, 16, WIDTH)
        for k in (4, 3, 5, 2, 6, 1, 7):
            y_send[c, k - 1] = encode(y_sum[c, lax.rem(y + k, 8)])
            y_copy(c, k).start()

    each(over_y)

    first_load.wait()
    second_load.wait()

    def adam(c):
        grad = y_sum[c, y]
        for k in range(1, 8):
            y_copy(c, k).wait_recv()
            grad += decode(y_recv[c, k - 1])
        new_first = beta_first * first[:, columns(c)] + (1.0 - beta_first) * grad
        new_second = beta_second * second[:, columns(c)] + (1.0 - beta_second) * grad * grad
        first_out[:, columns(c)] = new_first
        second_out[:, columns(c)] = new_second
        first_hat = new_first / (1.0 - beta_first**STEP)
        second_hat = new_second / (1.0 - beta_second**STEP)
        low[c, z] = (first_hat / (jnp.sqrt(second_hat) + adam_eps)).astype(BF16)
        for k in (4, 3, 5, 2, 6, 1, 7):
            low_copy(c, k).start()

    each(adam)

    total[...] = jnp.zeros_like(total)

    def expand(c):
        for k in range(1, 8):
            low_copy(c, k).wait_recv()
        total[...] += lax.dot_general(
            low[c].reshape(128, WIDTH), basis[c], (((1,), (1,)), ((), ())), preferred_element_type=F32
        )

    each(expand)
    d_send[...] = total[...].astype(BF16).reshape(8, 16, 1024)
    for k in (4, 3, 5, 2, 6, 1, 7):
        d_copy(k).start()

    weight_load.wait()

    def update(block, delta):
        place = pl.ds(pl.multiple_of(block * 1024, 1024), 1024)
        value = weight[:, place].astype(F32) - step_rate * delta.astype(F32)
        weight_out[:, place] = value.astype(BF16)

    update(z, d_send[z])
    for k in (1, 7, 2, 6, 3, 5, 4):
        d_copy(k).wait_recv()
        update(along_z(-k), d_recv[k - 1])

    def drain(c):
        for o in PARENT:
            rs_copy(c, o).wait_send()
            ag_copy(c, o).wait_send()
        core_copy(c).wait_send()
        for k in range(1, 4):
            x_copy(c, k).wait_send()
        for k in range(1, 8):
            y_copy(c, k).wait_send()
            low_copy(c, k).wait_send()

    each(drain)
    for k in range(1, 8):
        d_copy(k).wait_send()


def body(activations, cotangent, basis, weight, first_moment, second_moment):
    vmem, dma = pltpu.VMEM, pltpu.SemaphoreType.DMA
    return pl.pallas_call(
        kernel,
        out_shape=(
            jax.ShapeDtypeStruct((16, 8192), BF16),
            jax.ShapeDtypeStruct((16, 1024), F32),
            jax.ShapeDtypeStruct((16, 1024), F32),
        ),
        in_specs=[pl.BlockSpec(memory_space=pl.ANY)] * 6,
        out_specs=(pl.BlockSpec(memory_space=pltpu.VMEM),) * 3,
        scratch_shapes=[
            vmem((512, 1024), BF16),
            vmem((512, 1024), BF16),
            vmem((CHUNKS, 1024, WIDTH), BF16),
            vmem((16, 8192), BF16),
            vmem((16, 1024), F32),
            vmem((16, 1024), F32),
            vmem((CHUNKS, 8, 64, WIDTH), F32),
            vmem((CHUNKS, 7, 64, WIDTH), BF16),
            vmem((CHUNKS, 7, 64, WIDTH), BF16),
            vmem((CHUNKS, 8, 64, WIDTH), BF16),
            vmem((2, 4, 8, 16, 512), BF16),
            vmem((CHUNKS, 4, 128, WIDTH), F32),
            vmem((CHUNKS, 4, 128, WIDTH), F32),
            vmem((CHUNKS, 4, 128, WIDTH), F32),
            vmem((CHUNKS, 3, 128, WIDTH), BF16),
            vmem((CHUNKS, 3, 128, WIDTH), BF16),
            vmem((CHUNKS, 8, 16, WIDTH), F32),
            vmem((CHUNKS, 7, 16, WIDTH), BF16),
            vmem((CHUNKS, 7, 16, WIDTH), BF16),
            vmem((CHUNKS, 8, 16, WIDTH), BF16),
            vmem((128, 1024), F32),
            vmem((8, 16, 1024), BF16),
            vmem((7, 16, 1024), BF16),
            dma((5 + CHUNKS,)),
            dma((CHUNKS, 7)),
            dma((CHUNKS, 7)),
            dma((CHUNKS, 7)),
            dma((CHUNKS, 7)),
            dma((CHUNKS,)),
            dma((CHUNKS,)),
            dma((CHUNKS, 3)),
            dma((CHUNKS, 3)),
            dma((CHUNKS, 7)),
            dma((CHUNKS, 7)),
            dma((CHUNKS, 7)),
            dma((CHUNKS, 7)),
            dma((7,)),
            dma((7,)),
        ],
        compiler_params=pltpu.CompilerParams(
            collective_id=1, has_side_effects=True, vmem_limit_bytes=48 * 2**20
        ),
        name="galore_step",
    )(activations, cotangent, basis, weight, first_moment, second_moment)


def solution(mesh):
    rows = P(("mp", "dp"), None)
    return jax.shard_map(
        body,
        mesh=mesh,
        in_specs=(P("dp", "mp"), P("dp", "mp"), P("mp", None), rows, rows, rows),
        out_specs=(rows, rows, rows),
        check_vma=False,
    )
```

time: 298 us -> 87.1 us (0.29)
  the two profiles are of different devices: /device:TPU:16 before, /device:TPU:8 now
where the time goes in v1:
time: 87.1 us; the launch traced here: 86.8 us
  Pallas kernels  77.5 us (89%)
  local copies, waits for them, and re-layouts  8.62 us (10%)
    pallas_call x1, Pallas kernels, body(): pl.pallas_call(kernel, out_shape=(jax.ShapeDtypeStruct((16, 8192), BF16),...  77.5 us
    unnamed x15, local copies, waits for them, and re-layouts  8.62 us

profile of v1, /device:TPU:8, one launch (start us, length us, event | category | flops | bytes accessed | tf_op | source)
XLA Modules:
  0.0 86.8 jit_solution(11615127880734948326)
XLA Ops:
  0.6 0.0 copy-start
  0.6 1.6 %copy-done = bf16[1024,1024]{1,0:T(8,128)(2,1)S(1)} copy-done((bf16[1024,1024]{1,0:T(8,128)(2,1)S(1)}, bf16[1024,1024]{1,0:T(8,128)(2,1)}, u32[]{:S(2)}) %copy-start) | copy-done | bytes 2097176
  2.2 0.0 copy-start.1
  2.2 1.2 %copy-done.1 = bf16[512,1024]{1,0:T(8,128)(2,1)S(1)} copy-done((bf16[512,1024]{1,0:T(8,128)(2,1)S(1)}, bf16[512,1024]{1,0:T(8,128)(2,1)}, u32[]{:S(2)}) %copy-start.1) | copy-done | bytes 1048600
  3.4 0.0 copy-start.2
  3.5 1.2 %copy-done.2 = bf16[512,1024]{1,0:T(8,128)(2,1)S(1)} copy-done((bf16[512,1024]{1,0:T(8,128)(2,1)S(1)}, bf16[512,1024]{1,0:T(8,128)(2,1)}, u32[]{:S(2)}) %copy-start.2) | copy-done | bytes 1048600
  4.7 0.0 copy-start.3
  4.7 0.9 %copy-done.3 = bf16[16,8192]{1,0:T(8,128)(2,1)S(1)} copy-done((bf16[16,8192]{1,0:T(8,128)(2,1)S(1)}, bf16[16,8192]{1,0:T(8,128)(2,1)}, u32[]{:S(2)}) %copy-start.3) | copy-done | bytes 262168
  5.6 0.0 copy-start.4
  5.6 0.8 copy-done.4
  6.5 0.0 copy-start.5
  6.5 0.8 copy-done.5
  7.3 77.5 %galore_step.1 = (bf16[16,8192]{1,0:T(8,128)(2,1)S(1)}, f32[16,1024]{1,0:T(8,128)S(1)}, f32[16,1024]{1,0:T(8,128)S(1)}) custom-call(bf16[512,1024]{1,0:T(8,128)(2,1)S(1)} %copy-done.1, bf16[512,1024]{1,0:T(8,128)(2,1)S(1)} %copy-done.2, bf16[1024,1024]{1,0:T(8,128)(2,1)S(1)} %copy-done, bf16[16,8192]{1,0:T(8,128)(2,1)S(1)} %copy-done.3, ...), custom_call_target="tpu_custom_call" | custom-call | tf_op jit(solution)/shard_map/galore_step/pallas_call | solution.py:309
  84.8 0.7 copy.12
  85.5 0.6 copy.13
  86.1 0.6 copy.14
Async XLA Ops:
  0.6 1.6 %copy-start = (bf16[1024,1024]{1,0:T(8,128)(2,1)S(1)}, bf16[1024,1024]{1,0:T(8,128)(2,1)}, u32[]{:S(2)}) copy-start(bf16[1024,1024]{1,0:T(8,128)(2,1)} %basis_in.1) | copy-start | bytes 6291460
  2.2 1.2 %copy-start.1 = (bf16[512,1024]{1,0:T(8,128)(2,1)S(1)}, bf16[512,1024]{1,0:T(8,128)(2,1)}, u32[]{:S(2)}) copy-start(bf16[512,1024]{1,0:T(8,128)(2,1)} %act_in.1) | copy-start | bytes 3145732
  3.4 1.2 %copy-start.2 = (bf16[512,1024]{1,0:T(8,128)(2,1)S(1)}, bf16[512,1024]{1,0:T(8,128)(2,1)}, u32[]{:S(2)}) copy-start(bf16[512,1024]{1,0:T(8,128)(2,1)} %cot_in.1) | copy-start | bytes 3145732
  4.7 0.9 %copy-start.3 = (bf16[16,8192]{1,0:T(8,128)(2,1)S(1)}, bf16[16,8192]{1,0:T(8,128)(2,1)}, u32[]{:S(2)}) copy-start(bf16[16,8192]{1,0:T(8,128)(2,1)} %weight_in.1) | copy-start | bytes 786436
  5.6 0.8 copy-start.4
  6.5 0.8 copy-start.5

commit v2 on v1

v2 whole, which is shorter than its diff:
```python
import functools

import jax
import jax.numpy as jnp
from jax import lax
from jax.experimental import pallas as pl
from jax.experimental.pallas import tpu as pltpu
from jax.sharding import PartitionSpec as P

STEP = 1000

beta_first = 0.9
beta_second = 0.999
adam_eps = 1e-08
step_rate = 0.1

MESH = pl.DeviceIdType.MESH
F32, BF16 = jnp.float32, jnp.bfloat16

TREES = (
    {4: 2, 3: 2, 2: 0, 1: 0, -3: -2, -2: 0, -1: 0},
    {4: 3, 3: 2, 2: 1, 1: 0, -3: -2, -2: -1, -1: 0},
)
SLOT = {o: i for i, o in enumerate((3, 1, -3, -1, 4, 2, -2))}
JOINED = (((3, 1), (-3, -1)), ())
CHUNKS = 4
AHEAD = 1
GROUPS = 4
EACH = CHUNKS // GROUPS
WIDTH = 1024 // CHUNKS
WIDE = 1024 // GROUPS
LIFT = 2.0**24


def children(tree, node):
    return [o for o in tree if tree[o] == node]


def height(tree, node):
    return 1 + max([height(tree, o) for o in children(tree, node)], default=-1)


def depth(tree, node):
    return 0 if node == 0 else 1 + depth(tree, tree[node])


def encode(value):
    return ((value * value) * (value * jnp.abs(value))).astype(BF16)


def decode(code):
    code = code.astype(F32)
    root = lax.rsqrt(jnp.maximum(jnp.abs(code), 1e-37))
    return code * (root * root) * lax.rsqrt(root)


def each(function, count=CHUNKS):
    lax.fori_loop(0, count, lambda c, carry: (function(c), carry)[1], 0)


def kernel(
    act_in, cot_in, basis_in, weight_in, first_in, second_in,
    weight_out, first_out, second_out,
    act, cot, basis, weight, first, second,
    partial, rs_send, rs_recv, proj, act_t, own, core_send, core_recv,
    x_send, x_recv, y_sum, y_send, y_recv, low, total, d_send, d_recv,
    load_sem, rs_ss, rs_rs, ag_ss, ag_rs, core_ss, core_rs, x_ss, x_rs, y_ss, y_rs, low_ss, low_rs, d_ss, d_rs,
    near_sem, far_sem,
):
    dp, z = lax.axis_index("dp"), lax.axis_index("mp")
    y, x, core = dp // 8, (dp // 2) % 4, dp % 2
    sign = 1 - 2 * core

    def along_z(offset):
        return lax.rem(z + sign * offset + 16, 8)

    def at(y_to, x_to, core_to, z_to):
        return ((y_to * 4 + x_to) * 2 + core_to, z_to)

    def z_peer(offset):
        return at(y, x, core, along_z(offset))

    def x_peer(k):
        return at(y, lax.rem(x + k, 4), core, z)

    def y_peer(k):
        return at(lax.rem(y + k, 8), x, core, z)

    core_peer = at(y, x, 1 - core, z)

    def columns(c):
        return pl.ds(pl.multiple_of(c * WIDTH, WIDTH), WIDTH)

    barrier = pltpu.get_barrier_semaphore()
    peers = [z_peer(k) for k in (1, -1, 2, -2)] + [core_peer] + [x_peer(k) for k in (1, 3, 2)]
    peers += [y_peer(k) for k in (1, 7)]
    for peer in peers:
        pl.semaphore_signal(barrier, inc=1, device_id=peer, device_id_type=MESH)

    def wide(g):
        return pl.ds(pl.multiple_of(g * WIDE, WIDE), WIDE)

    def load(i, source, target):
        return pltpu.make_async_copy(source, target, load_sem.at[i])

    cot_load = load(0, cot_in, cot)
    act_load = load(1, act_in, act)
    weight_load = load(2, weight_in, weight)
    first_load = load(3, first_in, first)
    second_load = load(4, second_in, second)

    def basis_load(c):
        return load(5 + c, basis_in.at[:, columns(c)], basis.at[c])

    cot_load.start()
    each(lambda c: basis_load(c).start())
    act_load.start()
    first_load.start()
    second_load.start()
    weight_load.start()

    def send(source, target, send_sem, recv_sem, peer):
        return pltpu.make_async_remote_copy(
            src_ref=source,
            dst_ref=target,
            send_sem=send_sem,
            recv_sem=recv_sem,
            device_id=peer,
            device_id_type=MESH,
        )

    def rs_copy(tree, c, o, size=1):
        i = SLOT[o]
        place = pl.ds(i, size)
        return send(
            rs_send.at[c, place], rs_recv.at[c, place], rs_ss.at[c, i], rs_rs.at[c, i], z_peer(tree[o] - o)
        )

    def ag_copy(tree, c, o):
        i, block = SLOT[o], along_z(-tree[o])
        return send(proj.at[c, block], proj.at[c, block], ag_ss.at[c, i], ag_rs.at[c, i], z_peer(o - tree[o]))

    def core_copy(c):
        return send(core_send.at[c], core_recv.at[c], core_ss.at[c], core_rs.at[c], core_peer)

    def x_copy(c, k):
        return send(x_send.at[c, k - 1], x_recv.at[c, k - 1], x_ss.at[c], x_rs.at[c], x_peer(k))

    def x_all(c):
        return send(x_send.at[c], x_recv.at[c], x_ss.at[c], x_rs.at[c], x_peer(1))

    def y_copy(g, k):
        return send(y_send.at[g, k - 1], y_recv.at[g, k - 1], y_ss.at[g], y_rs.at[g], y_peer(k))

    def y_all(g):
        return send(y_send.at[g], y_recv.at[g], y_ss.at[g], y_rs.at[g], y_peer(1))

    def low_copy(g, k):
        return send(low.at[g, z], low.at[g, z], low_ss.at[g], low_rs.at[g], z_peer(k))

    def low_all(g):
        seven = low.at[g, pl.ds(0, 7)]
        return send(seven, seven, low_ss.at[g], low_rs.at[g], z_peer(1))

    def d_copy(k):
        return send(d_send.at[along_z(k)], d_recv.at[k - 1], d_ss.at[k - 1], d_rs.at[k - 1], z_peer(k))

    def multiply(c):
        basis_load(c).wait()
        product = jnp.dot(cot[...], basis[c], preferred_element_type=F32)
        partial[c] = (product * LIFT).reshape(8, 64, WIDTH)

    def meet(semaphore, distance):
        for k in (distance, 8 - distance):
            pl.semaphore_signal(semaphore, inc=1, device_id=y_peer(k), device_id_type=MESH)
        pl.semaphore_wait(semaphore, 2)

    def transpose(i):
        block = act[:, pl.ds(pl.multiple_of(i * 128, 128), 128)].T.reshape(4, 2, 16, 512)
        for j in range(4):
            for k in range(2):
                act_t[k, j, i] = block[j, k]

    def project(tree, joined):
        size = {o: 1 for o in tree} | {pair[0]: 2 for pair in joined}
        second = {pair[1]: pair[0] for pair in joined}
        seen = set()

        def arrived(c, o):
            first = second.get(o, o)
            if first not in seen:
                rs_copy(tree, c, first, size[first]).wait_recv()
            return decode(rs_recv[c, SLOT[o]])

        def note(nodes):
            seen.update(second.get(o, o) for o in nodes)

        def rs_step(c, o):
            value = partial[c, along_z(-o)]
            for child in children(tree, o):
                value += arrived(c, child)
            rs_send[c, SLOT[o]] = encode(value)

        def rs_start(c, o):
            if o not in second:
                rs_copy(tree, c, o, size[o]).start()

        def first_sends(c):
            @pl.when(c > 0)
            def _():
                multiply(c)

            for o in [o for o in tree if height(tree, o) == 0]:
                rs_step(c, o)
                if size[o] == 1 and o not in second:
                    rs_copy(tree, c, o).start()
                elif o in second:
                    rs_copy(tree, c, second[o], 2).start()

        each(first_sends)
        act_load.wait()
        lax.fori_loop(0, 8, lambda i, carry: (transpose(i), carry)[1], 0)
        meet(near_sem, 1)

        for level in range(1, height(tree, 0)):

            nodes = [o for o in tree if height(tree, o) == level]

            def later_sends(c):
                for o in nodes:
                    rs_step(c, o)
                    rs_start(c, o)

            each(later_sends)
            note(child for o in nodes for child in children(tree, o))

        meet(far_sem, 2)

        def own_block(c):
            value = partial[c, z]
            for child in children(tree, 0):
                value += arrived(c, child)
            proj[c, z] = (value * (1.0 / LIFT)).astype(BF16)
            for o in children(tree, 0):
                ag_copy(tree, c, o).start()

        each(own_block)

        for level in range(1, max(depth(tree, o) for o in tree)):

            def forward(c):
                for o in tree:
                    if depth(tree, o) == level and children(tree, o):
                        ag_copy(tree, c, o).wait_recv()
                        for child in children(tree, o):
                            ag_copy(tree, c, child).start()

            each(forward)

    def wait_leaves(tree, c):
        for o in tree:
            if not children(tree, o):
                ag_copy(tree, c, o).wait_recv()

    cot_load.wait()
    multiply(0)
    pl.semaphore_wait(barrier, len(peers))

    for number, tree in enumerate(TREES):
        pl.when(core == number)(functools.partial(project, tree, JOINED[number]))

    def gradient(c):
        for number, tree in enumerate(TREES):
            pl.when(core == number)(functools.partial(wait_leaves, tree, c))
        here = proj[c].reshape(512, WIDTH)
        other = jnp.dot(act_t[1 - core].reshape(512, 512), here, preferred_element_type=F32)
        core_send[c] = other.reshape(4, 128, WIDTH)
        core_copy(c).start()
        mine = jnp.dot(act_t[core].reshape(512, 512), here, preferred_element_type=F32)
        own[c] = mine.reshape(4, 128, WIDTH)

    def over_x(c):
        core_copy(c).wait_recv()
        for k in (2, 1, 3):
            to = lax.rem(x + k, 4)
            x_send[c, k - 1] = encode(own[c, to] + core_recv[c, to])
            x_copy(c, k).start()

    def gradient_and_x(c):
        over_x(c)

        @pl.when(c + AHEAD < CHUNKS)
        def _():
            gradient(c + AHEAD)

    for c in range(AHEAD):
        gradient(c)
    each(gradient_and_x)

    def over_y(g):
        for j in range(EACH):
            c = g * EACH + j
            value = own[c, x] + core_recv[c, x]
            x_all(c).wait_recv()
            for k in range(1, 4):
                value += decode(x_recv[c, k - 1])
            y_sum[g, :, :, j * WIDTH : (j + 1) * WIDTH] = value.reshape(8, 16, WIDTH)
        for k in (4, 3, 5, 2, 6, 1, 7):
            y_send[g, k - 1] = encode(y_sum[g, lax.rem(y + k, 8)])
            y_copy(g, k).start()

    each(over_y, GROUPS)

    first_load.wait()
    second_load.wait()

    def adam(g):
        grad = y_sum[g, y]
        y_all(g).wait_recv()
        for k in range(1, 8):
            grad += decode(y_recv[g, k - 1])
        new_first = beta_first * first[:, wide(g)] + (1.0 - beta_first) * grad
        new_second = beta_second * second[:, wide(g)] + (1.0 - beta_second) * grad * grad
        first_out[:, wide(g)] = new_first
        second_out[:, wide(g)] = new_second
        first_hat = new_first / (1.0 - beta_first**STEP)
        second_hat = new_second / (1.0 - beta_second**STEP)
        low[g, z] = (first_hat / (jnp.sqrt(second_hat) + adam_eps)).astype(BF16)
        for k in (4, 3, 5, 2, 6, 1, 7):
            low_copy(g, k).start()

    each(adam, GROUPS)

    total[...] = jnp.zeros_like(total)

    def expand(g):
        low_all(g).wait_recv()
        for j in range(EACH):
            total[...] += lax.dot_general(
                low[g, :, :, j * WIDTH : (j + 1) * WIDTH].reshape(128, WIDTH),
                basis[g * EACH + j],
                (((1,), (1,)), ((), ())),
                preferred_element_type=F32,
            )

    each(expand, GROUPS)
    d_send[...] = total[...].astype(BF16).reshape(8, 16, 1024)
    for k in (4, 3, 5, 2, 6, 1, 7):
        d_copy(k).start()

    def drain_z(tree, joined, c):
        size = {o: 1 for o in tree} | {pair[0]: 2 for pair in joined} | {pair[1]: 0 for pair in joined}
        for o in tree:
            if size[o]:
                rs_copy(tree, c, o, size[o]).wait_send()
            ag_copy(tree, c, o).wait_send()

    def drain(c):
        for number, tree in enumerate(TREES):
            pl.when(core == number)(functools.partial(drain_z, tree, JOINED[number], c))
        core_copy(c).wait_send()
        x_all(c).wait_send()

    def drain_group(g):
        y_all(g).wait_send()
        low_all(g).wait_send()

    each(drain)
    each(drain_group, GROUPS)

    weight_load.wait()

    def update(block, delta):
        place = pl.ds(pl.multiple_of(block * 1024, 1024), 1024)
        value = weight[:, place].astype(F32) - step_rate * delta.astype(F32)
        weight_out[:, place] = value.astype(BF16)

    update(z, d_send[z])
    for k in (1, 7, 2, 6, 3, 5, 4):
        d_copy(k).wait_recv()
        update(along_z(-k), d_recv[k - 1])
    for k in range(1, 8):
        d_copy(k).wait_send()


def store(weight, first, second, weight_out, first_out, second_out, sem):
    copies = [
        pltpu.make_async_copy(source, target, sem.at[i])
        for i, (source, target) in enumerate(((weight, weight_out), (first, first_out), (second, second_out)))
    ]
    for copy in copies:
        copy.start()
    for copy in copies:
        copy.wait()


def body(activations, cotangent, basis, weight, first_moment, second_moment):
    vmem, dma = pltpu.VMEM, pltpu.SemaphoreType.DMA
    results = pl.pallas_call(
        kernel,
        out_shape=(vmem((16, 8192), BF16), vmem((16, 1024), F32), vmem((16, 1024), F32)),
        in_specs=[pl.BlockSpec(memory_space=pltpu.HBM)] * 6,
        out_specs=(pl.BlockSpec(memory_space=pltpu.VMEM),) * 3,
        scratch_shapes=[
            vmem((512, 1024), BF16),
            vmem((512, 1024), BF16),
            vmem((CHUNKS, 1024, WIDTH), BF16),
            vmem((16, 8192), BF16),
            vmem((16, 1024), F32),
            vmem((16, 1024), F32),
            vmem((CHUNKS, 8, 64, WIDTH), F32),
            vmem((CHUNKS, 7, 64, WIDTH), BF16),
            vmem((CHUNKS, 7, 64, WIDTH), BF16),
            vmem((CHUNKS, 8, 64, WIDTH), BF16),
            vmem((2, 4, 8, 16, 512), BF16),
            vmem((CHUNKS, 4, 128, WIDTH), F32),
            vmem((CHUNKS, 4, 128, WIDTH), F32),
            vmem((CHUNKS, 4, 128, WIDTH), F32),
            vmem((CHUNKS, 3, 128, WIDTH), BF16),
            vmem((CHUNKS, 3, 128, WIDTH), BF16),
            vmem((GROUPS, 8, 16, WIDE), F32),
            vmem((GROUPS, 7, 16, WIDE), BF16),
            vmem((GROUPS, 7, 16, WIDE), BF16),
            vmem((GROUPS, 8, 16, WIDE), BF16),
            vmem((128, 1024), F32),
            vmem((8, 16, 1024), BF16),
            vmem((7, 16, 1024), BF16),
            dma((5 + CHUNKS,)),
            dma((CHUNKS, 7)),
            dma((CHUNKS, 7)),
            dma((CHUNKS, 7)),
            dma((CHUNKS, 7)),
            dma((CHUNKS,)),
            dma((CHUNKS,)),
            dma((CHUNKS,)),
            dma((CHUNKS,)),
            dma((GROUPS,)),
            dma((GROUPS,)),
            dma((GROUPS,)),
            dma((GROUPS,)),
            dma((7,)),
            dma((7,)),
            pltpu.SemaphoreType.REGULAR,
            pltpu.SemaphoreType.REGULAR,
        ],
        compiler_params=pltpu.CompilerParams(
            collective_id=1, has_side_effects=True, vmem_limit_bytes=60 * 2**20
        ),
        name="galore_step",
    )(activations, cotangent, basis, weight, first_moment, second_moment)
    return pl.pallas_call(
        store,
        out_shape=tuple(jax.ShapeDtypeStruct(r.shape, r.dtype) for r in results),
        in_specs=[pl.BlockSpec(memory_space=pltpu.VMEM)] * 3,
        out_specs=(pl.BlockSpec(memory_space=pltpu.HBM),) * 3,
        scratch_shapes=[dma((3,))],
        compiler_params=pltpu.CompilerParams(vmem_limit_bytes=2 * 2**20),
        name="store_results",
    )(*results)


def solution(mesh):
    rows = P(("mp", "dp"), None)
    return jax.shard_map(
        body,
        mesh=mesh,
        in_specs=(P("dp", "mp"), P("dp", "mp"), P("mp", None), rows, rows, rows),
        out_specs=(rows, rows, rows),
        check_vma=False,
    )
```

time: 87.1 us -> 73.6 us (0.85)
  local copies, waits for them, and re-layouts: 8.62 us -> 0 us
  Pallas kernels: 77.5 us -> 72.8 us
    unnamed x15 -> x0, local copies, waits for them, and re-layouts: 8.62 us -> none
    pallas_call x1 -> x2, Pallas kernels: 77.5 us -> 72.8 us  [the longest x1 72.1 us: body(): pl.pallas_call(kernel, out_shape=(vmem((16, 8192), BF16), vmem((16, 1024)...]
where the time goes in v2:
time: 73.6 us; the launch traced here: 73.5 us
  Pallas kernels  72.8 us (99%)
    pallas_call x1, Pallas kernels, body(): pl.pallas_call(kernel, out_shape=(vmem((16, 8192), BF16), vmem((16, 1024)...  72.1 us

profile of v2, /device:TPU:8, one launch (start us, length us, event | category | flops | bytes accessed | tf_op | source)
XLA Modules:
  0.0 73.5 jit_solution(17337728173008114312)
XLA Ops:
  0.6 72.1 %galore_step.1 = (bf16[16,8192]{1,0:T(8,128)(2,1)S(1)}, f32[16,1024]{1,0:T(8,128)S(1)}, f32[16,1024]{1,0:T(8,128)S(1)}) custom-call(bf16[512,1024]{1,0:T(8,128)(2,1)} %act_in.1, bf16[512,1024]{1,0:T(8,128)(2,1)} %cot_in.1, bf16[1024,1024]{1,0:T(8,128)(2,1)} %basis_in.1, bf16[16,8192]{1,0:T(8,128)(2,1)} %weight_in.1, f32[16,1024]{1,0:T(8,128)} %first_in.1, ...), custom_call_target="tpu_custom_call" | custom-call | tf_op jit(solution)/shard_map/galore_step/pallas_call | solution.py:399
  72.7 0.8 %store_results.1 = (bf16[16,8192]{1,0:T(8,128)(2,1)}, f32[16,1024]{1,0:T(8,128)}, f32[16,1024]{1,0:T(8,128)}) custom-call(bf16[16,8192]{1,0:T(8,128)(2,1)S(1)} %get-tuple-element.6.weight, f32[16,1024]{1,0:T(8,128)S(1)} %get-tuple-element.7.first, f32[16,1024]{1,0:T(8,128)S(1)} %get-tuple-element.8.second), custom_call_target="tpu_custom_call" | custom-call | tf_op jit(solution)/shard_map/store_results/pallas_call | solution.py:451

commit v3 on v2

v3 whole, which is shorter than its diff:
```python
import functools

import jax
import jax.numpy as jnp
from jax import lax
from jax.experimental import pallas as pl
from jax.experimental.pallas import tpu as pltpu
from jax.sharding import PartitionSpec as P

STEP = 1000

beta_first = 0.9
beta_second = 0.999
adam_eps = 1e-08
step_rate = 0.1

MESH = pl.DeviceIdType.MESH
F32, BF16 = jnp.float32, jnp.bfloat16

TREES = (
    {4: 2, 3: 2, 2: 0, 1: 0, -3: -2, -2: 0, -1: 0},
    {4: 3, 3: 2, 2: 1, 1: 0, -3: -2, -2: -1, -1: 0},
)
SLOT = {o: i for i, o in enumerate(TREES[0])}
CHUNKS = 4
WIDTH = 1024 // CHUNKS
LIFT = 2.0**24
RING = (0, 1, 7, 2, 6, 3, 5, 4)
NEAR = 5


def children(tree, node):
    return [o for o in tree if tree[o] == node]


def height(tree, node):
    return 1 + max([height(tree, o) for o in children(tree, node)], default=-1)


def depth(tree, node):
    return 0 if node == 0 else 1 + depth(tree, tree[node])


def encode(value):
    return ((value * value) * (value * jnp.abs(value))).astype(BF16)


def decode(code):
    code = code.astype(F32)
    root = lax.rsqrt(jnp.maximum(jnp.abs(code), 1e-37))
    return code * (root * root) * lax.rsqrt(root)


def each(function, count=CHUNKS):
    lax.fori_loop(0, count, lambda c, carry: (function(c), carry)[1], 0)


def kernel(
    act_in, cot_in, basis_in, weight_in, first_in, second_in,
    weight_out, first_out, second_out,
    act, cot, basis, weight, first, second,
    partial, rs_send, rs_recv, proj, act_t, own, core_send, core_recv,
    x_send, x_recv, y_sum, y_send, y_recv, yf_send, yf_recv, xf_sum, xf_send, xf_recv, low, total, d_send, d_recv,
    load_sem, rs_ss, rs_rs, ag_ss, ag_rs, core_ss, core_rs, x_ss, x_rs, y_ss, y_rs, low_ss, low_rs, d_ss, d_rs,
    f_sem, near_sem, far_sem,
):
    dp, z = lax.axis_index("dp"), lax.axis_index("mp")
    y, x, core = dp // 8, (dp // 2) % 4, dp % 2
    sign = 1 - 2 * core

    def along_z(offset):
        return lax.rem(z + sign * offset + 16, 8)

    def at(y_to, x_to, core_to, z_to):
        return ((y_to * 4 + x_to) * 2 + core_to, z_to)

    def z_peer(offset):
        return at(y, x, core, along_z(offset))

    def x_peer(k):
        return at(y, lax.rem(x + k, 4), core, z)

    def y_peer(k):
        return at(lax.rem(y + k, 8), x, core, z)

    core_peer = at(y, x, 1 - core, z)

    def columns(c):
        return pl.ds(pl.multiple_of(c * WIDTH, WIDTH), WIDTH)

    barrier = pltpu.get_barrier_semaphore()
    peers = [z_peer(k) for k in (1, -1, 2, -2)] + [core_peer] + [x_peer(k) for k in (1, 3, 2)]
    peers += [y_peer(k) for k in (1, 7)]
    for peer in peers:
        pl.semaphore_signal(barrier, inc=1, device_id=peer, device_id_type=MESH)

    def load(i, source, target):
        return pltpu.make_async_copy(source, target, load_sem.at[i])

    cot_load = load(0, cot_in, cot)
    act_load = load(1, act_in, act)
    weight_load = load(2, weight_in, weight)
    first_load = load(3, first_in, first)
    second_load = load(4, second_in, second)

    def basis_load(c):
        return load(5 + c, basis_in.at[:, columns(c)], basis.at[c])

    cot_load.start()
    each(lambda c: basis_load(c).start())
    act_load.start()
    first_load.start()
    second_load.start()
    weight_load.start()

    def send(source, target, send_sem, recv_sem, peer):
        return pltpu.make_async_remote_copy(
            src_ref=source,
            dst_ref=target,
            send_sem=send_sem,
            recv_sem=recv_sem,
            device_id=peer,
            device_id_type=MESH,
        )

    def rs_copy(tree, c, o):
        i = SLOT[o]
        return send(rs_send.at[c, i], rs_recv.at[c, i], rs_ss.at[c, i], rs_rs.at[c, i], z_peer(tree[o] - o))

    def ag_copy(tree, c, o):
        i, block = SLOT[o], along_z(-tree[o])
        return send(proj.at[c, block], proj.at[c, block], ag_ss.at[c, i], ag_rs.at[c, i], z_peer(o - tree[o]))

    def core_copy(c):
        return send(core_send.at[c], core_recv.at[c], core_ss.at[c], core_rs.at[c], core_peer)

    def x_copy(c, k):
        return send(x_send.at[c, k - 1], x_recv.at[c, k - 1], x_ss.at[c], x_rs.at[c], x_peer(k))

    def x_all(c):
        return send(x_send.at[c], x_recv.at[c], x_ss.at[c], x_rs.at[c], x_peer(1))

    def y_copy(c, k):
        return send(y_send.at[c, k - 1], y_recv.at[c, k - 1], y_ss.at[c], y_rs.at[c], y_peer(k))

    def y_all(c):
        return send(y_send.at[c], y_recv.at[c], y_ss.at[c], y_rs.at[c], y_peer(1))

    def yf_copy(k):
        return send(yf_send.at[k - 1], yf_recv.at[k - 1], f_sem.at[0], f_sem.at[1], y_peer(k))

    def yf_all():
        return send(yf_send, yf_recv, f_sem.at[0], f_sem.at[1], y_peer(1))

    def xf_copy(k):
        return send(xf_send.at[k - 1], xf_recv.at[k - 1], f_sem.at[2], f_sem.at[3], x_peer(k))

    def xf_all():
        return send(xf_send, xf_recv, f_sem.at[2], f_sem.at[3], x_peer(1))

    def low_copy(c, i):
        part = int(i >= NEAR)
        return send(low.at[c, 0], low.at[c, i], low_ss.at[c], low_rs.at[c, part], z_peer(RING[i]))

    def low_part(c, part):
        some = low.at[c, pl.ds(*((1, NEAR - 1), (NEAR, 8 - NEAR))[part])]
        return send(some, some, low_ss.at[c], low_rs.at[c, part], z_peer(1))

    def d_copy(i):
        return send(d_send.at[i], d_recv.at[i - 1], d_ss.at[i - 1], d_rs.at[i - 1], z_peer(-RING[i]))

    def multiply(c):
        basis_load(c).wait()
        product = jnp.dot(cot[...], basis[c], preferred_element_type=F32)
        partial[c] = (product * LIFT).reshape(8, 64, WIDTH)

    def greet(semaphore, distance):
        for k in (distance, 8 - distance):
            pl.semaphore_signal(semaphore, inc=1, device_id=y_peer(k), device_id_type=MESH)

    def transpose(i):
        block = act[:, pl.ds(pl.multiple_of(i * 128, 128), 128)].T.reshape(4, 2, 16, 512)
        for j in range(4):
            for k in range(2):
                act_t[k, j, i] = block[j, k]

    def project(tree):
        late = [o for o in (1, -1) if tree[o] == 0 and height(tree, o) == 0]

        def arrived(c, o):
            rs_copy(tree, c, o).wait_recv()
            return decode(rs_recv[c, SLOT[o]])

        def rs_step(c, o):
            value = partial[c, along_z(-o)]
            for child in children(tree, o):
                value += arrived(c, child)
            rs_send[c, SLOT[o]] = encode(value)
            rs_copy(tree, c, o).start()

        def first_sends(c):
            @pl.when(c > 0)
            def _():
                multiply(c)

            for o in [o for o in tree if height(tree, o) == 0 and o not in late]:
                rs_step(c, o)

        each(first_sends)
        act_load.wait()
        lax.fori_loop(0, 8, lambda i, carry: (transpose(i), carry)[1], 0)
        greet(near_sem, 1)

        for level in range(1, height(tree, 0)):

            nodes = [o for o in tree if height(tree, o) == level] + [o for o in late if level == 1]

            def later_sends(c):
                for o in nodes:
                    rs_step(c, o)

            each(later_sends)

        def own_block(c):
            value = partial[c, z]
            for child in children(tree, 0):
                value += arrived(c, child)
            proj[c, z] = (value * (1.0 / LIFT)).astype(BF16)
            for o in children(tree, 0):
                ag_copy(tree, c, o).start()

        each(own_block)

        for level in range(1, max(depth(tree, o) for o in tree)):

            def forward(c):
                for o in tree:
                    if depth(tree, o) == level and children(tree, o):
                        ag_copy(tree, c, o).wait_recv()
                        for child in children(tree, o):
                            ag_copy(tree, c, child).start()

            each(forward)

    def wait_leaves(tree, c):
        for o in tree:
            if not children(tree, o):
                ag_copy(tree, c, o).wait_recv()

    cot_load.wait()
    multiply(0)
    pl.semaphore_wait(barrier, len(peers))

    for number, tree in enumerate(TREES):
        pl.when(core == number)(functools.partial(project, tree))

    def gradient(c):
        for number, tree in enumerate(TREES):
            pl.when(core == number)(functools.partial(wait_leaves, tree, c))
        here = proj[c].reshape(512, WIDTH)
        other = jnp.dot(act_t[1 - core].reshape(512, 512), here, preferred_element_type=F32)
        core_send[c] = other.reshape(4, 8, 16, WIDTH)
        core_copy(c).start()
        mine = jnp.dot(act_t[core].reshape(512, 512), here, preferred_element_type=F32)
        own[c] = mine.reshape(4, 8, 16, WIDTH)

    def y_first():
        core_copy(0).wait_recv()
        for k in (4, 3, 5, 2, 6, 1, 7):
            to = lax.rem(y + k, 8)
            yf_send[k - 1] = encode(own[0, :, to] + core_recv[0, :, to])
            yf_copy(k).start()

    def over_x(c):
        core_copy(c).wait_recv()
        for k in (2, 1, 3):
            to = lax.rem(x + k, 4)
            x_send[c, k - 1] = encode(own[c, to] + core_recv[c, to])
            x_copy(c, k).start()

    def over_y(c):
        value = own[c, x] + core_recv[c, x]
        x_all(c).wait_recv()
        for k in range(1, 4):
            value += decode(x_recv[c, k - 1])
        y_sum[c] = value
        for k in (4, 3, 5, 2, 6, 1, 7):
            y_send[c, k - 1] = encode(y_sum[c, lax.rem(y + k, 8)])
            y_copy(c, k).start()

    def x_second():
        value = own[0, :, y] + core_recv[0, :, y]
        yf_all().wait_recv()
        for k in range(1, 8):
            value += decode(yf_recv[k - 1])
        xf_sum[...] = value
        for k in (2, 1, 3):
            xf_send[k - 1] = encode(xf_sum[lax.rem(x + k, 4)])
            xf_copy(k).start()

    pl.semaphore_wait(near_sem, 2)
    greet(far_sem, 2)
    gradient(0)
    pl.semaphore_wait(far_sem, 2)
    y_first()

    def gradient_and_x(i):
        gradient(i + 1)
        over_x(i + 1)

    each(gradient_and_x, CHUNKS - 1)

    each(lambda i: over_y(i + 1), CHUNKS - 2)
    x_second()
    over_y(CHUNKS - 1)

    first_load.wait()
    second_load.wait()

    def grad_first():
        xf_all().wait_recv()
        grad = xf_sum[x]
        for k in range(1, 4):
            grad += decode(xf_recv[k - 1])
        return grad

    def grad_other(c):
        y_all(c).wait_recv()
        grad = y_sum[c, y]
        for k in range(1, 8):
            grad += decode(y_recv[c, k - 1])
        return grad

    def adam(c, grad):
        new_first = beta_first * first[:, columns(c)] + (1.0 - beta_first) * grad
        new_second = beta_second * second[:, columns(c)] + (1.0 - beta_second) * grad * grad
        first_out[:, columns(c)] = new_first
        second_out[:, columns(c)] = new_second
        first_hat = new_first / (1.0 - beta_first**STEP)
        second_hat = new_second / (1.0 - beta_second**STEP)
        low[c, 0] = (first_hat / (jnp.sqrt(second_hat) + adam_eps)).astype(BF16)
        for i in range(7, 0, -1):
            low_copy(c, i).start()

    each(lambda i: adam(i + 1, grad_other(i + 1)), CHUNKS - 2)
    adam(0, grad_first())
    adam(CHUNKS - 1, grad_other(CHUNKS - 1))

    def expand(start, size, part):
        rows = slice(16 * start, 16 * (start + size))
        total[rows] = jnp.zeros((16 * size, 1024), F32)

        def add(i):
            c = (i + 1) % (CHUNKS - 1) + (CHUNKS - 2) * (i // (CHUNKS - 1))
            low_part(c, part).wait_recv()
            total[rows] += lax.dot_general(
                low[c, start : start + size].reshape(16 * size, WIDTH),
                basis[c],
                (((1,), (1,)), ((), ())),
                preferred_element_type=F32,
            )

        each(add)
        d_send[start : start + size] = total[rows].astype(BF16).reshape(size, 16, 1024)
        for i in range(start + size - 1, max(start, 1) - 1, -1):
            d_copy(i).start()

    expand(0, NEAR, 0)
    expand(NEAR, 8 - NEAR, 1)

    def drain_z(tree, c):
        for o in tree:
            rs_copy(tree, c, o).wait_send()
            ag_copy(tree, c, o).wait_send()

    def drain(c):
        for number, tree in enumerate(TREES):
            pl.when(core == number)(functools.partial(drain_z, tree, c))
        core_copy(c).wait_send()
        low_part(c, 0).wait_send()
        low_part(c, 1).wait_send()

        @pl.when(c > 0)
        def _():
            x_all(c).wait_send()
            y_all(c).wait_send()

    each(drain)
    yf_all().wait_send()
    xf_all().wait_send()

    weight_load.wait()

    def update(block, delta):
        place = pl.ds(pl.multiple_of(block * 1024, 1024), 1024)
        value = weight[:, place].astype(F32) - step_rate * delta.astype(F32)
        weight_out[:, place] = value.astype(BF16)

    update(z, d_send[0])
    for i in range(1, 8):
        d_copy(i).wait_recv()
        update(along_z(RING[i]), d_recv[i - 1])
    for i in range(1, 8):
        d_copy(i).wait_send()


def store(weight, first, second, weight_out, first_out, second_out, sem):
    copies = [
        pltpu.make_async_copy(source, target, sem.at[i])
        for i, (source, target) in enumerate(((weight, weight_out), (first, first_out), (second, second_out)))
    ]
    for copy in copies:
        copy.start()
    for copy in copies:
        copy.wait()


def body(activations, cotangent, basis, weight, first_moment, second_moment):
    vmem, dma = pltpu.VMEM, pltpu.SemaphoreType.DMA
    results = pl.pallas_call(
        kernel,
        out_shape=(vmem((16, 8192), BF16), vmem((16, 1024), F32), vmem((16, 1024), F32)),
        in_specs=[pl.BlockSpec(memory_space=pltpu.HBM)] * 6,
        out_specs=(pl.BlockSpec(memory_space=pltpu.VMEM),) * 3,
        scratch_shapes=[
            vmem((512, 1024), BF16),
            vmem((512, 1024), BF16),
            vmem((CHUNKS, 1024, WIDTH), BF16),
            vmem((16, 8192), BF16),
            vmem((16, 1024), F32),
            vmem((16, 1024), F32),
            vmem((CHUNKS, 8, 64, WIDTH), F32),
            vmem((CHUNKS, 7, 64, WIDTH), BF16),
            vmem((CHUNKS, 7, 64, WIDTH), BF16),
            vmem((CHUNKS, 8, 64, WIDTH), BF16),
            vmem((2, 4, 8, 16, 512), BF16),
            vmem((CHUNKS, 4, 8, 16, WIDTH), F32),
            vmem((CHUNKS, 4, 8, 16, WIDTH), F32),
            vmem((CHUNKS, 4, 8, 16, WIDTH), F32),
            vmem((CHUNKS, 3, 8, 16, WIDTH), BF16),
            vmem((CHUNKS, 3, 8, 16, WIDTH), BF16),
            vmem((CHUNKS, 8, 16, WIDTH), F32),
            vmem((CHUNKS, 7, 16, WIDTH), BF16),
            vmem((CHUNKS, 7, 16, WIDTH), BF16),
            vmem((7, 4, 16, WIDTH), BF16),
            vmem((7, 4, 16, WIDTH), BF16),
            vmem((4, 16, WIDTH), F32),
            vmem((3, 16, WIDTH), BF16),
            vmem((3, 16, WIDTH), BF16),
            vmem((CHUNKS, 8, 16, WIDTH), BF16),
            vmem((128, 1024), F32),
            vmem((8, 16, 1024), BF16),
            vmem((7, 16, 1024), BF16),
            dma((5 + CHUNKS,)),
            dma((CHUNKS, 7)),
            dma((CHUNKS, 7)),
            dma((CHUNKS, 7)),
            dma((CHUNKS, 7)),
            dma((CHUNKS,)),
            dma((CHUNKS,)),
            dma((CHUNKS,)),
            dma((CHUNKS,)),
            dma((CHUNKS,)),
            dma((CHUNKS,)),
            dma((CHUNKS,)),
            dma((CHUNKS, 2)),
            dma((7,)),
            dma((7,)),
            dma((4,)),
            pltpu.SemaphoreType.REGULAR,
            pltpu.SemaphoreType.REGULAR,
        ],
        compiler_params=pltpu.CompilerParams(
            collective_id=1, has_side_effects=True, vmem_limit_bytes=60 * 2**20
        ),
        name="galore_step",
    )(activations, cotangent, basis, weight, first_moment, second_moment)
    return pl.pallas_call(
        store,
        out_shape=tuple(jax.ShapeDtypeStruct(r.shape, r.dtype) for r in results),
        in_specs=[pl.BlockSpec(memory_space=pltpu.VMEM)] * 3,
        out_specs=(pl.BlockSpec(memory_space=pltpu.HBM),) * 3,
        scratch_shapes=[dma((3,))],
        compiler_params=pltpu.CompilerParams(vmem_limit_bytes=2 * 2**20),
        name="store_results",
    )(*results)


def solution(mesh):
    rows = P(("mp", "dp"), None)
    return jax.shard_map(
        body,
        mesh=mesh,
        in_specs=(P("dp", "mp"), P("dp", "mp"), P("mp", None), rows, rows, rows),
        out_specs=(rows, rows, rows),
        check_vma=False,
    )
```

time: 73.6 us -> 72.2 us (0.981)
  the two profiles are of different devices: /device:TPU:8 before, /device:TPU:64 now
where the time goes in v3:
time: 72.2 us; the launch traced here: 72.1 us
  Pallas kernels  71.4 us (99%)
    pallas_call x1, Pallas kernels, body(): pl.pallas_call(kernel, out_shape=(vmem((16, 8192), BF16), vmem((16, 1024)...  70.7 us

profile of v3, /device:TPU:64, one launch (start us, length us, event | category | flops | bytes accessed | tf_op | source)
XLA Modules:
  0.0 72.1 jit_solution(4794387672927970754)
XLA Ops:
  0.6 70.7 %galore_step.1 = (bf16[16,8192]{1,0:T(8,128)(2,1)S(1)}, f32[16,1024]{1,0:T(8,128)S(1)}, f32[16,1024]{1,0:T(8,128)S(1)}) custom-call(bf16[512,1024]{1,0:T(8,128)(2,1)} %act_in.1, bf16[512,1024]{1,0:T(8,128)(2,1)} %cot_in.1, bf16[1024,1024]{1,0:T(8,128)(2,1)} %basis_in.1, bf16[16,8192]{1,0:T(8,128)(2,1)} %weight_in.1, f32[16,1024]{1,0:T(8,128)} %first_in.1, ...), custom_call_target="tpu_custom_call" | custom-call | tf_op jit(solution)/shard_map/galore_step/pallas_call | solution.py:420
  71.3 0.8 %store_results.1 = (bf16[16,8192]{1,0:T(8,128)(2,1)}, f32[16,1024]{1,0:T(8,128)}, f32[16,1024]{1,0:T(8,128)}) custom-call(bf16[16,8192]{1,0:T(8,128)(2,1)S(1)} %get-tuple-element.6.weight, f32[16,1024]{1,0:T(8,128)S(1)} %get-tuple-element.7.first, f32[16,1024]{1,0:T(8,128)S(1)} %get-tuple-element.8.second), custom_call_target="tpu_custom_call" | custom-call | tf_op jit(solution)/shard_map/store_results/pallas_call | solution.py:478

commit v4 on v3

--- a/solution.py
+++ b/solution.py
@@ -89,7 +89,7 @@
         return pl.ds(pl.multiple_of(c * WIDTH, WIDTH), WIDTH)
 
     barrier = pltpu.get_barrier_semaphore()
-    peers = [z_peer(k) for k in (1, -1, 2, -2)] + [core_peer] + [x_peer(k) for k in (1, 3, 2)]
+    peers = [z_peer(k) for k in (2, -2, 1, -1)] + [core_peer] + [x_peer(k) for k in (1, 3, 2)]
     peers += [y_peer(k) for k in (1, 7)]
     for peer in peers:
         pl.semaphore_signal(barrier, inc=1, device_id=peer, device_id_type=MESH)
@@ -227,7 +227,8 @@
                 value += arrived(c, child)
             proj[c, z] = (value * (1.0 / LIFT)).astype(BF16)
             for o in children(tree, 0):
-                ag_copy(tree, c, o).start()
+                if o not in late:
+                    ag_copy(tree, c, o).start()
 
         each(own_block)
 
@@ -239,6 +240,9 @@
                         ag_copy(tree, c, o).wait_recv()
                         for child in children(tree, o):
                             ag_copy(tree, c, child).start()
+                if level == 1:
+                    for o in late:
+                        ag_copy(tree, c, o).start()
 
             each(forward)
 

time: 72.2 us -> 72 us (level)
  the two profiles are of different devices: /device:TPU:64 before, /device:TPU:16 now
where the time goes in v4:
time: 72 us; the launch traced here: 71.8 us
  Pallas kernels  71.2 us (99%)
    pallas_call x1, Pallas kernels, body(): pl.pallas_call(kernel, out_shape=(vmem((16, 8192), BF16), vmem((16, 1024)...  70.4 us

profile of v4, /device:TPU:16, one launch (start us, length us, event | category | flops | bytes accessed | tf_op | source)
XLA Modules:
  0.0 71.8 jit_solution(5004368754643323155)
XLA Ops:
  0.6 70.4 %galore_step.1 = (bf16[16,8192]{1,0:T(8,128)(2,1)S(1)}, f32[16,1024]{1,0:T(8,128)S(1)}, f32[16,1024]{1,0:T(8,128)S(1)}) custom-call(bf16[512,1024]{1,0:T(8,128)(2,1)} %act_in.1, bf16[512,1024]{1,0:T(8,128)(2,1)} %cot_in.1, bf16[1024,1024]{1,0:T(8,128)(2,1)} %basis_in.1, bf16[16,8192]{1,0:T(8,128)(2,1)} %weight_in.1, f32[16,1024]{1,0:T(8,128)} %first_in.1, ...), custom_call_target="tpu_custom_call" | custom-call | tf_op jit(solution)/shard_map/galore_step/pallas_call | solution.py:424
  71.1 0.8 %store_results.1 = (bf16[16,8192]{1,0:T(8,128)(2,1)}, f32[16,1024]{1,0:T(8,128)}, f32[16,1024]{1,0:T(8,128)}) custom-call(bf16[16,8192]{1,0:T(8,128)(2,1)S(1)} %get-tuple-element.6.weight, f32[16,1024]{1,0:T(8,128)S(1)} %get-tuple-element.7.first, f32[16,1024]{1,0:T(8,128)S(1)} %get-tuple-element.8.second), custom_call_target="tpu_custom_call" | custom-call | tf_op jit(solution)/shard_map/store_results/pallas_call | solution.py:482

commit v5 on v4

--- a/solution.py
+++ b/solution.py
@@ -263,7 +263,7 @@
             pl.when(core == number)(functools.partial(wait_leaves, tree, c))
         here = proj[c].reshape(512, WIDTH)
         other = jnp.dot(act_t[1 - core].reshape(512, 512), here, preferred_element_type=F32)
-        core_send[c] = other.reshape(4, 8, 16, WIDTH)
+        core_send[c] = encode(other).reshape(4, 8, 16, WIDTH)
         core_copy(c).start()
         mine = jnp.dot(act_t[core].reshape(512, 512), here, preferred_element_type=F32)
         own[c] = mine.reshape(4, 8, 16, WIDTH)
@@ -272,18 +272,18 @@
         core_copy(0).wait_recv()
         for k in (4, 3, 5, 2, 6, 1, 7):
             to = lax.rem(y + k, 8)
-            yf_send[k - 1] = encode(own[0, :, to] + core_recv[0, :, to])
+            yf_send[k - 1] = encode(own[0, :, to] + decode(core_recv[0, :, to]))
             yf_copy(k).start()
 
     def over_x(c):
         core_copy(c).wait_recv()
         for k in (2, 1, 3):
             to = lax.rem(x + k, 4)
-            x_send[c, k - 1] = encode(own[c, to] + core_recv[c, to])
+            x_send[c, k - 1] = encode(own[c, to] + decode(core_recv[c, to]))
             x_copy(c, k).start()
 
     def over_y(c):
-        value = own[c, x] + core_recv[c, x]
+        value = own[c, x] + decode(core_recv[c, x])
         x_all(c).wait_recv()
         for k in range(1, 4):
             value += decode(x_recv[c, k - 1])
@@ -293,7 +293,7 @@
             y_copy(c, k).start()
 
     def x_second():
-        value = own[0, :, y] + core_recv[0, :, y]
+        value = own[0, :, y] + decode(core_recv[0, :, y])
         yf_all().wait_recv()
         for k in range(1, 8):
             value += decode(yf_recv[k - 1])
@@ -439,8 +439,8 @@
             vmem((CHUNKS, 8, 64, WIDTH), BF16),
             vmem((2, 4, 8, 16, 512), BF16),
             vmem((CHUNKS, 4, 8, 16, WIDTH), F32),
-            vmem((CHUNKS, 4, 8, 16, WIDTH), F32),
-            vmem((CHUNKS, 4, 8, 16, WIDTH), F32),
+            vmem((CHUNKS, 4, 8, 16, WIDTH), BF16),
+            vmem((CHUNKS, 4, 8, 16, WIDTH), BF16),
             vmem((CHUNKS, 3, 8, 16, WIDTH), BF16),
             vmem((CHUNKS, 3, 8, 16, WIDTH), BF16),
             vmem((CHUNKS, 8, 16, WIDTH), F32),

time: 72 us -> 71.7 us (level)
  the two profiles are of different devices: /device:TPU:16 before, /device:TPU:64 now
where the time goes in v5:
time: 71.7 us; the launch traced here: 71.6 us
  Pallas kernels  70.9 us (99%)
    pallas_call x1, Pallas kernels, body(): pl.pallas_call(kernel, out_shape=(vmem((16, 8192), BF16), vmem((16, 1024)...  70.2 us

profile of v5, /device:TPU:64, one launch (start us, length us, event | category | flops | bytes accessed | tf_op | source)
XLA Modules:
  0.0 71.6 jit_solution(12538177791539712642)
XLA Ops:
  0.6 70.2 %galore_step.1 = (bf16[16,8192]{1,0:T(8,128)(2,1)S(1)}, f32[16,1024]{1,0:T(8,128)S(1)}, f32[16,1024]{1,0:T(8,128)S(1)}) custom-call(bf16[512,1024]{1,0:T(8,128)(2,1)} %act_in.1, bf16[512,1024]{1,0:T(8,128)(2,1)} %cot_in.1, bf16[1024,1024]{1,0:T(8,128)(2,1)} %basis_in.1, bf16[16,8192]{1,0:T(8,128)(2,1)} %weight_in.1, f32[16,1024]{1,0:T(8,128)} %first_in.1, ...), custom_call_target="tpu_custom_call" | custom-call | tf_op jit(solution)/shard_map/galore_step/pallas_call | solution.py:424
  70.8 0.8 %store_results.1 = (bf16[16,8192]{1,0:T(8,128)(2,1)}, f32[16,1024]{1,0:T(8,128)}, f32[16,1024]{1,0:T(8,128)}) custom-call(bf16[16,8192]{1,0:T(8,128)(2,1)S(1)} %get-tuple-element.6.weight, f32[16,1024]{1,0:T(8,128)S(1)} %get-tuple-element.7.first, f32[16,1024]{1,0:T(8,128)S(1)} %get-tuple-element.8.second), custom_call_target="tpu_custom_call" | custom-call | tf_op jit(solution)/shard_map/store_results/pallas_call | solution.py:482
